TPU v7x, 32 devices: a whole 2x2x4 slice. The times are simulated.
32 devices in a mesh: dp: 4 (over y, x), fsdp: 8 (over z, core).
Axes of the slice: x: 2, y: 2, z: 4, core: 2. Of those that a mesh axis runs over, the one named last changes fastest.
Arguments:
- tokens: bfloat16 [32, 1024, 768], P(('dp', 'fsdp')), may hold values from -6 to 6
- row_lengths: int32 [32], P(('dp', 'fsdp')), may hold values from 256 to 1024, as said below
- live_mask: int32 [2, 32, 1024], P(None, ('dp', 'fsdp')), may hold values 0 or 1
- pass_index: int32 [32], P(('dp', 'fsdp')), may hold values from 1 to 4
- w_qkv: bfloat16 [768, 2304], P(None, ('dp', 'fsdp')), may hold values from -0.21875 to 0.21875
- w_out: bfloat16 [768, 768], P(None, ('dp', 'fsdp')), may hold values from -2.5 to 2.5
- w_up: bfloat16 [768, 3072], P(None, ('dp', 'fsdp')), may hold values from -0.21875 to 0.21875
- w_down: bfloat16 [3072, 768], P(('dp', 'fsdp')), may hold values from -0.109375 to 0.109375
- norm_gains: bfloat16 [2, 768], P(None, ('dp', 'fsdp')), may hold values from 0.099609375 to 1.8984375
- norm_shifts: bfloat16 [2, 768], P(None, ('dp', 'fsdp')), may hold values from -4 to 4
- pass_table: bfloat16 [5, 768], P(None, ('dp', 'fsdp')), may hold values from -6 to 6
- cotangent: float32 [32, 1024, 768], P(('dp', 'fsdp')), may hold values from -6 to 6
Outputs:
- activations: bfloat16 [32, 1024, 768], P(('dp', 'fsdp'))
- input_grad: float32 [32, 1024, 768], P(('dp', 'fsdp'))
- grad_qkv: float32 [768, 2304], P(None, ('dp', 'fsdp'))
- grad_out: float32 [768, 768], P(None, ('dp', 'fsdp'))
- grad_up: float32 [768, 3072], P(None, ('dp', 'fsdp'))
- grad_down: float32 [3072, 768], P(('dp', 'fsdp'))
- grad_gains: float32 [2, 768], P(None, ('dp', 'fsdp'))
- grad_shifts: float32 [768], P(('dp', 'fsdp'))
- grad_second_shift: float32 [768], P(('dp', 'fsdp'))
- grad_table: float32 [5, 768], P(None, ('dp', 'fsdp'))
Inputs may be any that keep to these rules, and one draw needn't show every extreme that they name: `row_lengths`: some row uses all 1024 positions and some row only 256.
All inputs are finite; a program needn't handle non-finite values. No bound on the sum of `live_mask` on one device may be relied on, other than what follows from the above.
Results may differ from a plain program's by a relative error of at most 0.015.
Values may be sent and summed in bfloat16 or wider, within the bound.
No kernel may reach another device: no remote copies, remote signals or barrier semaphores. Data moves between devices by JAX's collectives and lax.ppermute only.
A program may use at most 320 MiB of HBM per device.

v0:
```python
import jax
import jax.numpy as jnp
from jax import lax
from jax.sharding import PartitionSpec as P

HEADS = 12
HEAD = 64


norm_epsilon = 1e-05
masked_score = -1000000000.0


def norm_apply(values, gain, shift):
    center = jnp.mean(values, axis=-1, keepdims=True)
    centered = values - center
    spread = jnp.mean(centered * centered, axis=-1, keepdims=True)
    return centered * lax.rsqrt(spread + norm_epsilon) * gain + shift


def smooth_gate(values):
    return jax.nn.gelu(values, approximate=True)


def weight_grad(left_side, right_side):
    return jnp.einsum("rsa,rsb->ab", left_side, right_side, preferred_element_type=jnp.float32)


def block_scores(query_rows, key_heads, first_row, live_flags):
    seq_length = key_heads.shape[0]
    scores = (
        jnp.einsum("qhe,khe->hqk", query_rows, key_heads, preferred_element_type=jnp.float32)
        * 0.125
    )
    positions = jnp.arange(seq_length, dtype=jnp.int32)
    query_pos = first_row + jnp.arange(query_rows.shape[0], dtype=jnp.int32)
    visible = (positions[None, :] <= query_pos[:, None]) & (
        (live_flags[None, :] > 0.5) | (positions[None, :] == query_pos[:, None])
    )
    return (jnp.where(visible[None], scores, masked_score), visible)


def attend_forward(query_heads, key_heads, value_heads, live_flags):
    seq_length = query_heads.shape[0]
    block_rows = min(512, seq_length)

    def one_block(block_index):
        first_row = block_index * block_rows
        query_rows = lax.dynamic_slice_in_dim(query_heads, first_row, block_rows, 0)
        scores, visible = block_scores(query_rows, key_heads, first_row, live_flags)
        row_top = jnp.max(scores, axis=-1, keepdims=True)
        weights = jnp.exp(scores - row_top)
        row_total = jnp.sum(weights, axis=-1, keepdims=True)
        soft_low = (weights / row_total).astype(jnp.bfloat16)
        mixed_rows = jnp.einsum(
            "hqk,khe->qhe", soft_low, value_heads, preferred_element_type=jnp.float32
        )
        return (mixed_rows, (row_top + jnp.log(row_total))[..., 0])

    block_outputs, log_totals = lax.map(
        one_block, jnp.arange(seq_length // block_rows, dtype=jnp.int32)
    )
    return (block_outputs.reshape(query_heads.shape), log_totals)


def attend_backward(query_heads, key_heads, value_heads, live_flags, log_totals, out_grad):
    seq_length = query_heads.shape[0]
    block_rows = min(512, seq_length)

    def one_block(carry, block_index):
        key_grad, value_grad = carry
        first_row = block_index * block_rows
        query_rows = lax.dynamic_slice_in_dim(query_heads, first_row, block_rows, 0)
        grad_rows = lax.dynamic_slice_in_dim(out_grad, first_row, block_rows, 0)
        scores, visible = block_scores(query_rows, key_heads, first_row, live_flags)
        soft = jnp.where(visible[None], jnp.exp(scores - log_totals[block_index][..., None]), 0.0)
        soft_low = soft.astype(jnp.bfloat16)
        soft_grad = jnp.einsum(
            "qhe,khe->hqk", grad_rows, value_heads, preferred_element_type=jnp.float32
        )
        row_dot = jnp.sum(soft * soft_grad, axis=-1, keepdims=True)
        score_grad = (soft * (soft_grad - row_dot)).astype(jnp.bfloat16)
        query_grad = (
            jnp.einsum("hqk,khe->qhe", score_grad, key_heads, preferred_element_type=jnp.float32)
            * 0.125
        )
        key_grad = (
            key_grad
            + jnp.einsum("hqk,qhe->khe", score_grad, query_rows, preferred_element_type=jnp.float32)
            * 0.125
        )
        value_grad = value_grad + jnp.einsum(
            "hqk,qhe->khe", soft_low, grad_rows, preferred_element_type=jnp.float32
        )
        return ((key_grad, value_grad), query_grad)

    empty_grad = jnp.zeros(key_heads.shape, jnp.float32)
    (key_grad, value_grad), query_blocks = lax.scan(
        one_block, (empty_grad, empty_grad), jnp.arange(seq_length // block_rows, dtype=jnp.int32)
    )
    return (query_blocks.reshape(query_heads.shape), key_grad, value_grad)


def layer_forward(inputs, live_flags, params):
    w_qkv, w_out, w_up, w_down, gains, shifts = params
    row_count, seq_length, width = inputs.shape
    normed = norm_apply(inputs, gains[0], shifts[0]).astype(jnp.bfloat16)
    mixed = jnp.dot(normed, w_qkv, preferred_element_type=jnp.float32).astype(jnp.bfloat16)
    split_heads = mixed.reshape(row_count, seq_length, 3, HEADS, HEAD)

    def per_row(parts):
        return attend_forward(parts[0], parts[1], parts[2], parts[3])

    attended, log_totals = lax.map(
        per_row, (split_heads[:, :, 0], split_heads[:, :, 1], split_heads[:, :, 2], live_flags)
    )
    attended = attended.reshape(row_count, seq_length, width).astype(jnp.bfloat16)
    branch = jnp.dot(attended, w_out, preferred_element_type=jnp.float32)
    hidden = inputs + live_flags[..., None] * branch
    second = norm_apply(hidden, gains[1], shifts[1]).astype(jnp.bfloat16)
    lifted = jnp.dot(second, w_up, preferred_element_type=jnp.float32)
    activated = smooth_gate(lifted).astype(jnp.bfloat16)
    result = hidden + live_flags[..., None] * jnp.dot(
        activated, w_down, preferred_element_type=jnp.float32
    )
    kept = (inputs, normed, mixed, log_totals, attended, hidden, second, lifted, activated)
    return (result, kept)


def layer_backward(grad_given, live_flags, params, kept):
    w_qkv, w_out, w_up, w_down, gains, shifts = params
    inputs, normed, mixed, log_totals, attended, hidden, second, lifted, activated = kept
    row_count, seq_length, width = inputs.shape
    live_cols = live_flags[..., None]
    drop_grad = (live_cols * grad_given).astype(jnp.bfloat16)
    down_grad = weight_grad(activated, drop_grad)
    act_grad = jnp.einsum("rsd,fd->rsf", drop_grad, w_down, preferred_element_type=jnp.float32)
    unused_value, gate_back = jax.vjp(smooth_gate, lifted)
    lift_grad = gate_back(act_grad)[0].astype(jnp.bfloat16)
    up_grad = weight_grad(second, lift_grad)
    second_grad = jnp.einsum("rsf,df->rsd", lift_grad, w_up, preferred_element_type=jnp.float32)
    unused_norm, later_back = jax.vjp(norm_apply, hidden, gains[1], shifts[1])
    through_norm, gain_later, shift_later = later_back(second_grad)
    hidden_grad = grad_given + through_norm
    branch_grad = (live_cols * hidden_grad).astype(jnp.bfloat16)
    out_grad = weight_grad(attended, branch_grad)
    attend_grad = jnp.einsum(
        "rsd,ed->rse", branch_grad, w_out, preferred_element_type=jnp.float32
    ).astype(jnp.bfloat16)
    split_heads = mixed.reshape(row_count, seq_length, 3, HEADS, HEAD)
    head_grads = attend_grad.reshape(row_count, seq_length, HEADS, HEAD)

    def per_row(parts):
        return attend_backward(parts[0], parts[1], parts[2], parts[3], parts[4], parts[5])

    query_grad, key_grad, value_grad = lax.map(
        per_row,
        (
            split_heads[:, :, 0],
            split_heads[:, :, 1],
            split_heads[:, :, 2],
            live_flags,
            log_totals,
            head_grads,
        ),
    )
    mixed_grad = (
        jnp.stack((query_grad, key_grad, value_grad), axis=2)
        .reshape(row_count, seq_length, 3 * width)
        .astype(jnp.bfloat16)
    )
    qkv_grad = weight_grad(normed, mixed_grad)
    normed_grad = jnp.einsum("rsc,dc->rsd", mixed_grad, w_qkv, preferred_element_type=jnp.float32)
    unused_first, first_back = jax.vjp(norm_apply, inputs, gains[0], shifts[0])
    through_first, gain_first, shift_first = first_back(normed_grad)
    inputs_grad = hidden_grad + through_first
    gain_grads = jnp.stack((gain_first, gain_later), axis=0)
    shift_grads = jnp.stack((shift_first, shift_later), axis=0)
    return (inputs_grad, (qkv_grad, out_grad, up_grad, down_grad, gain_grads, shift_grads))


def body(
    tokens,
    row_lengths,
    live_mask,
    pass_index,
    w_qkv,
    w_out,
    w_up,
    w_down,
    norm_gains,
    norm_shifts,
    pass_table,
    cotangent,
):
    seq_length = tokens.shape[1]
    positions = jnp.arange(seq_length, dtype=jnp.int32)
    inside = positions[None, :] < row_lengths[:, None]
    live_first = jnp.where(inside & (live_mask[0] > 0), 1.0, 0.0).astype(jnp.float32)
    live_later = jnp.where(inside & (live_mask[1] > 0), 1.0, 0.0).astype(jnp.float32)
    pass_count = pass_table.shape[0]
    pass_onehot = jnp.where(
        jnp.arange(pass_count, dtype=jnp.int32)[None, :] == pass_index[:, None], 1.0, 0.0
    ).astype(jnp.float32)

    def fetch():
        return (
            lax.all_gather(w_qkv, ("dp", "fsdp"), axis=1, tiled=True),
            lax.all_gather(w_out, ("dp", "fsdp"), axis=1, tiled=True),
            lax.all_gather(w_up, ("dp", "fsdp"), axis=1, tiled=True),
            lax.all_gather(w_down, ("dp", "fsdp"), axis=0, tiled=True),
            lax.all_gather(norm_gains, ("dp", "fsdp"), axis=1, tiled=True),
            lax.all_gather(norm_shifts, ("dp", "fsdp"), axis=1, tiled=True),
            lax.all_gather(pass_table, ("dp", "fsdp"), axis=1, tiled=True),
        )

    def block_params(fetched):
        return (
            fetched[0],
            fetched[1],
            fetched[2],
            fetched[3],
            fetched[4].astype(jnp.float32),
            fetched[5].astype(jnp.float32),
        )

    middle, kept_first = layer_forward(
        tokens.astype(jnp.float32), live_first, block_params(fetch())
    )
    fetched_later = fetch()
    embedding = jnp.dot(
        pass_onehot,
        fetched_later[6].astype(jnp.float32),
        precision=lax.Precision.HIGHEST,
        preferred_element_type=jnp.float32,
    )
    result, kept_later = layer_forward(
        middle + embedding[:, None, :], live_later, block_params(fetched_later)
    )
    later_grad, grads_later = layer_backward(
        cotangent, live_later, block_params(fetch()), kept_later
    )
    row_sums = jnp.sum(later_grad, axis=1)
    table_grad = jnp.einsum(
        "rp,rd->pd",
        pass_onehot,
        row_sums,
        precision=lax.Precision.HIGHEST,
        preferred_element_type=jnp.float32,
    )
    owned_later = (
        lax.psum_scatter(grads_later[0], ("dp", "fsdp"), scatter_dimension=1, tiled=True),
        lax.psum_scatter(grads_later[1], ("dp", "fsdp"), scatter_dimension=1, tiled=True),
        lax.psum_scatter(grads_later[2], ("dp", "fsdp"), scatter_dimension=1, tiled=True),
        lax.psum_scatter(grads_later[3], ("dp", "fsdp"), scatter_dimension=0, tiled=True),
        lax.psum_scatter(grads_later[4], ("dp", "fsdp"), scatter_dimension=1, tiled=True),
        lax.psum_scatter(grads_later[5], ("dp", "fsdp"), scatter_dimension=1, tiled=True),
        lax.psum_scatter(table_grad, ("dp", "fsdp"), scatter_dimension=1, tiled=True),
    )
    input_grad, grads_first = layer_backward(
        later_grad, live_first, block_params(fetch()), kept_first
    )
    owned_first = (
        lax.psum_scatter(grads_first[0], ("dp", "fsdp"), scatter_dimension=1, tiled=True),
        lax.psum_scatter(grads_first[1], ("dp", "fsdp"), scatter_dimension=1, tiled=True),
        lax.psum_scatter(grads_first[2], ("dp", "fsdp"), scatter_dimension=1, tiled=True),
        lax.psum_scatter(grads_first[3], ("dp", "fsdp"), scatter_dimension=0, tiled=True),
        lax.psum_scatter(grads_first[4], ("dp", "fsdp"), scatter_dimension=1, tiled=True),
        lax.psum_scatter(grads_first[5], ("dp", "fsdp"), scatter_dimension=1, tiled=True),
    )
    owned = tuple((owned_first[place] + owned_later[place] for place in range(6))) + (
        owned_later[6],
    )
    return (
        result.astype(jnp.bfloat16),
        input_grad,
        owned[0],
        owned[1],
        owned[2],
        owned[3],
        owned[4],
        owned[5][0],
        owned[5][1],
        owned[6],
    )


def solution(mesh):
    placed = (
        P(("dp", "fsdp"), None, None),
        P(("dp", "fsdp")),
        P(None, ("dp", "fsdp"), None),
        P(("dp", "fsdp")),
        P(None, ("dp", "fsdp")),
        P(None, ("dp", "fsdp")),
        P(None, ("dp", "fsdp")),
        P(("dp", "fsdp"), None),
        P(None, ("dp", "fsdp")),
        P(None, ("dp", "fsdp")),
        P(None, ("dp", "fsdp")),
        P(("dp", "fsdp"), None, None),
    )
    return jax.shard_map(
        body,
        mesh=mesh,
        in_specs=placed,
        out_specs=(
            P(("dp", "fsdp"), None, None),
            P(("dp", "fsdp"), None, None),
            P(None, ("dp", "fsdp")),
            P(None, ("dp", "fsdp")),
            P(None, ("dp", "fsdp")),
            P(("dp", "fsdp"), None),
            P(None, ("dp", "fsdp")),
            P(("dp", "fsdp")),
            P(("dp", "fsdp")),
            P(None, ("dp", "fsdp")),
        ),
        check_vma=False,
    )
```

profile of v0, /device:TPU:0, one launch (start us, length us, event | category | flops | bytes accessed | tf_op | source)
XLA Modules:
  0.0 1400.5 jit_solution(9389611113495994269)
XLA Ops:
  13.2 43.0 %all-gather = bf16[32,24,2]{1,2,0:T(2,128)(2,1)S(1)} all-gather(bf16[1,24,2]{1,2,0:T(2,128)(2,1)S(1)} %bitcast.322), channel_id=1, replica_groups=mesh['dp'=4,'fsdp'=8] {'dp','fsdp'}, dimensions={0}, use_global_device_ids=true | all-gather | bytes 3168 | tf_op jit(solution)/shard_map/all_gather | solution.py:212
  57.1 36.4 %all-gather.1 = bf16[32,24,2]{1,2,0:T(2,128)(2,1)S(1)} all-gather(bf16[1,24,2]{1,2,0:T(2,128)(2,1)S(1)} %bitcast.323), channel_id=1, replica_groups=mesh['dp'=4,'fsdp'=8] {'dp','fsdp'}, dimensions={0}, use_global_device_ids=true | all-gather | bytes 3168 | tf_op jit(solution)/shard_map/all_gather | solution.py:213
  95.8 38.9 %all-gather.2 = bf16[32,24,5]{1,2,0:T(8,128)(2,1)S(1)} all-gather(bf16[1,24,5]{1,2,0:T(8,128)(2,1)S(1)} %bitcast.321), channel_id=1, replica_groups=mesh['dp'=4,'fsdp'=8] {'dp','fsdp'}, dimensions={0}, use_global_device_ids=true | all-gather | bytes 7920 | tf_op jit(solution)/shard_map/all_gather | solution.py:214
  160.3 74.0 %while.94 = (s32[]{:T(128)}, bf16[2,512,12,64]{1,3,2,0:T(8,128)(2,1)}, f32[2,12,512]{2,1,0:T(8,128)S(1)}, s32[2]{0:T(128)S(1)}, f32[1024]{0:T(1024)S(1)}, /*inde...) while((s32[]{:T(128)}, ...), condition=%wide.region_5.6_spmd, body=%wide.region_2.5_spmd.sunk | while | flops 1688202752 | bytes 190286576 | solution.py:60
  172.7 13.0 fusion.221
  210.1 12.3 fusion.221
  293.4 73.1 %while.95 = (s32[]{:T(128)}, bf16[2,512,12,64]{1,3,2,0:T(8,128)(2,1)}, f32[2,12,512]{2,1,0:T(8,128)S(1)}, s32[2]{0:T(128)S(1)}, f32[1024]{0:T(1024)S(1)}, /*inde...) while((s32[]{:T(128)}, ...), condition=%wide.region_13.14_spmd, body=%wide.region_10.13_spmd.sunk | while | flops 1688202752 | bytes 190286576 | solution.py:60
  382.9 16.5 %fusion.71 = bf16[1024,3072]{1,0:T(8,128)(2,1)} fusion(f32[1024,3072]{1,0:T(8,128)} %fusion.120, bf16[3072,768]{1,0:T(8,128)(2,1)S(1)} %bitcast.325, f32[1,1024,768]{1,2,0:T(8,128)S(1)} %copy-done.22, f32[1024]{0:T(1024)S(1)} %get-tuple-element.1007), kind=kOutput, calls=%fused_computation.111 | convolution fusion | flops 4896325632 | bytes 26742784 | tf_op jit(solution)/shard_map/rsd,fd->rsf/dot_general | solution.py:137
  425.1 235.5 %while.96 = (s32[]{:T(128)}, f32[1024,12,64]{0,2,1:T(8,128)}, f32[1024,12,64]{0,2,1:T(8,128)}, bf16[2,512,12,64]{1,0,3,2:T(2,128)(2,1)}, s32[2]{0:T(128)S(1)}, /...) while((s32[]{:T(128)}, f32[1024,12,64]{0,2,1:T(8,128)}, ...), condition=%wide.region_20.21_spmd.clone, body=%wide.region_18.20_spmd.clone.sunk | while | flops 4146589184 | bytes 238479792 | solution.py:98
  439.6 19.1 %multiply_reduce_fusion.7 = (f32[12,512]{1,0:T(8,128)S(1)}, f32[12,512,1024]{2,1,0:T(8,128)}) fusion(f32[12,512]{1,0:T(8,128)S(1)} %dynamic-slice_bitcast_fusion.4, f32[12,512,1024]{2,1,0:T(8,128)} %fusion.236, pred[512,1024]{1,0:T(8,128)(4,1)S(1)} %fusion.237, bf16[1024,12,64]{0,2,1:T(8,128)(2,1)} %get-tuple-element.931, ...), kind=kOutput, calls=%fused_computation.39.clone.1 | convolution fusion | flops 843048960 | bytes 53264388 | tf_op jit(solution)/shard_map/while/body/eval_jaxpr/while/body/eval_jaxpr/qhe,khe->hqk/dot_general | solution.py:78
  458.7 21.4 %multiply_convert_fusion.14 = bf16[12,512,1024]{2,1,0:T(8,128)(2,1)} fusion(f32[12,512,1024]{2,1,0:T(8,128)} %get-tuple-element.802, f32[12,512]{1,0:T(8,128)S(1)} %get-tuple-element.803, f32[12,512]{1,0:T(8,128)S(1)} %dynamic-slice_bitcast_fusion.4, f32[12,512,1024]{2,1,0:T(8,128)} %fusion.236, pred[512,1024]{1,0:T(8,128)(4,1)S(1)} %fusion.237), kind=kLoop, calls=%fused_computation.38.clone.1 | loop fusion | flops 44040192 | bytes 63488000 | tf_op jit(solution)/shard_map/while/body/eval_jaxpr/while/body/eval_jaxpr/convert_element_type | solution.py:82
  492.0 27.1 %dynamic_update_slice.58 = bf16[2,512,12,64]{1,0,3,2:T(2,128)(2,1)} dynamic-update-slice(bf16[2,512,12,64]{1,0,3,2:T(2,128)(2,1)} %get-tuple-element.908, bf16[1,512,12,64]{1,0,3,2:T(2,128)(2,1)S(1)} %copy.153, s32[]{:T(128)} %get-tuple-element.905, s32[]{:T(128)} %constant.193.clone.1..sunk.2, s32[]{:T(128)} %constant.193.clone.1..sunk.2, s32[]{:T(128)} %constant.193.clone.1..sunk.2) | dynamic-update-slice | bytes 1572868 | tf_op jit(solution)/shard_map/while/body/eval_jaxpr/while/body/jit(dynamic_update_index_in_dim)/dynamic_update_slice | solution.py:60
  528.1 14.0 bitcast_add_fusion.12
  556.1 19.1 %multiply_reduce_fusion.7 = (f32[12,512]{1,0:T(8,128)S(1)}, f32[12,512,1024]{2,1,0:T(8,128)}) fusion(f32[12,512]{1,0:T(8,128)S(1)} %dynamic-slice_bitcast_fusion.4, f32[12,512,1024]{2,1,0:T(8,128)} %fusion.236, pred[512,1024]{1,0:T(8,128)(4,1)S(1)} %fusion.237, bf16[1024,12,64]{0,2,1:T(8,128)(2,1)} %get-tuple-element.931, ...), kind=kOutput, calls=%fused_computation.39.clone.1 | convolution fusion | flops 843048960 | bytes 53264388 | tf_op jit(solution)/shard_map/while/body/eval_jaxpr/while/body/eval_jaxpr/qhe,khe->hqk/dot_general | solution.py:78
  575.2 21.4 %multiply_convert_fusion.14 = bf16[12,512,1024]{2,1,0:T(8,128)(2,1)} fusion(f32[12,512,1024]{2,1,0:T(8,128)} %get-tuple-element.802, f32[12,512]{1,0:T(8,128)S(1)} %get-tuple-element.803, f32[12,512]{1,0:T(8,128)S(1)} %dynamic-slice_bitcast_fusion.4, f32[12,512,1024]{2,1,0:T(8,128)} %fusion.236, pred[512,1024]{1,0:T(8,128)(4,1)S(1)} %fusion.237), kind=kLoop, calls=%fused_computation.38.clone.1 | loop fusion | flops 44040192 | bytes 63488000 | tf_op jit(solution)/shard_map/while/body/eval_jaxpr/while/body/eval_jaxpr/convert_element_type | solution.py:82
  608.6 27.1 %dynamic_update_slice.58 = bf16[2,512,12,64]{1,0,3,2:T(2,128)(2,1)} dynamic-update-slice(bf16[2,512,12,64]{1,0,3,2:T(2,128)(2,1)} %get-tuple-element.908, bf16[1,512,12,64]{1,0,3,2:T(2,128)(2,1)S(1)} %copy.153, s32[]{:T(128)} %get-tuple-element.905, s32[]{:T(128)} %constant.193.clone.1..sunk.2, s32[]{:T(128)} %constant.193.clone.1..sunk.2, s32[]{:T(128)} %constant.193.clone.1..sunk.2) | dynamic-update-slice | bytes 1572868 | tf_op jit(solution)/shard_map/while/body/eval_jaxpr/while/body/jit(dynamic_update_index_in_dim)/dynamic_update_slice | solution.py:60
  645.5 14.9 %bitcast_add_fusion.12 = f32[1024,12,64]{0,2,1:T(8,128)} fusion(f32[1024,12,64]{0,2,1:T(8,128)} %get-tuple-element.907, f32[12,512]{1,0:T(8,128)S(1)} %dynamic-slice_bitcast_fusion.4, f32[12,512,1024]{2,1,0:T(8,128)} %fusion.236, pred[512,1024]{1,0:T(8,128)(4,1)S(1)} %copy-done.13, pred[]{:T(512)S(6)} %compare.6, ...), kind=kOutput, calls=%fused_computation.43.clone.1 | convolution fusion | flops 838336512 | bytes 32800772 | tf_op jit(solution)/shard_map/while/body/eval_jaxpr/while/body/eval_jaxpr/hqk,qhe->khe/dot_general | solution.py:92
  686.0 16.0 %fusion.64 = bf16[1024,3072]{1,0:T(8,128)(2,1)S(1)} fusion(f32[1024,3072]{1,0:T(8,128)} %fusion.126, bf16[3072,768]{1,0:T(8,128)(2,1)S(1)} %bitcast.327, f32[1,1024,768]{1,2,0:T(8,128)S(1)} %get-tuple-element.532, f32[1024]{0:T(1024)S(1)} %copy-done.57), kind=kOutput, calls=%fused_computation.104 | convolution fusion | flops 4896325632 | bytes 26742784 | tf_op jit(solution)/shard_map/rsd,fd->rsf/dot_general | solution.py:137
  735.7 238.3 %while.97 = (s32[]{:T(128)}, f32[1024,12,64]{0,2,1:T(8,128)}, f32[1024,12,64]{0,2,1:T(8,128)}, bf16[2,512,12,64]{1,0,3,2:T(2,128)(2,1)}, s32[2]{0:T(128)S(1)}, /...) while((s32[]{:T(128)}, f32[1024,12,64]{0,2,1:T(8,128)}, ...), condition=%wide.region_27.28_spmd.clone, body=%wide.region_25.27_spmd.clone.sunk | while | flops 4146589184 | bytes 225896816 | solution.py:98
  751.3 19.4 %multiply_reduce_fusion.8 = (f32[12,512]{1,0:T(8,128)S(1)}, f32[12,512,1024]{2,1,0:T(8,128)}) fusion(f32[12,512]{1,0:T(8,128)S(1)} %dynamic-slice_bitcast_fusion.5, f32[12,512,1024]{2,1,0:T(8,128)} %fusion.247, pred[512,1024]{1,0:T(8,128)(4,1)S(1)} %fusion.248, bf16[1024,12,64]{0,2,1:T(8,128)(2,1)} %get-tuple-element.979, ...), kind=kOutput, calls=%fused_computation.67.clone.1 | convolution fusion | flops 843048960 | bytes 53264388 | tf_op jit(solution)/shard_map/while/body/eval_jaxpr/while/body/eval_jaxpr/qhe,khe->hqk/dot_general | solution.py:78
  770.7 21.6 %multiply_convert_fusion.15 = bf16[12,512,1024]{2,1,0:T(8,128)(2,1)} fusion(f32[12,512,1024]{2,1,0:T(8,128)} %get-tuple-element.815, f32[12,512]{1,0:T(8,128)S(1)} %get-tuple-element.816, f32[12,512]{1,0:T(8,128)S(1)} %dynamic-slice_bitcast_fusion.5, f32[12,512,1024]{2,1,0:T(8,128)} %fusion.247, pred[512,1024]{1,0:T(8,128)(4,1)S(1)} %fusion.248), kind=kLoop, calls=%fused_computation.66.clone.1 | loop fusion | flops 44040192 | bytes 63488000 | tf_op jit(solution)/shard_map/while/body/eval_jaxpr/while/body/eval_jaxpr/convert_element_type | solution.py:82
  804.3 27.1 %dynamic_update_slice.59 = bf16[2,512,12,64]{1,0,3,2:T(2,128)(2,1)} dynamic-update-slice(bf16[2,512,12,64]{1,0,3,2:T(2,128)(2,1)} %get-tuple-element.956, bf16[1,512,12,64]{1,0,3,2:T(2,128)(2,1)S(1)} %copy.154, s32[]{:T(128)} %get-tuple-element.953, s32[]{:T(128)} %constant.193.clone.1..sunk.3, s32[]{:T(128)} %constant.193.clone.1..sunk.3, s32[]{:T(128)} %constant.193.clone.1..sunk.3) | dynamic-update-slice | bytes 1572868 | tf_op jit(solution)/shard_map/while/body/eval_jaxpr/while/body/jit(dynamic_update_index_in_dim)/dynamic_update_slice | solution.py:60
  840.3 13.8 bitcast_add_fusion.14
  869.4 19.2 %multiply_reduce_fusion.8 = (f32[12,512]{1,0:T(8,128)S(1)}, f32[12,512,1024]{2,1,0:T(8,128)}) fusion(f32[12,512]{1,0:T(8,128)S(1)} %dynamic-slice_bitcast_fusion.5, f32[12,512,1024]{2,1,0:T(8,128)} %fusion.247, pred[512,1024]{1,0:T(8,128)(4,1)S(1)} %fusion.248, bf16[1024,12,64]{0,2,1:T(8,128)(2,1)} %get-tuple-element.979, ...), kind=kOutput, calls=%fused_computation.67.clone.1 | convolution fusion | flops 843048960 | bytes 53264388 | tf_op jit(solution)/shard_map/while/body/eval_jaxpr/while/body/eval_jaxpr/qhe,khe->hqk/dot_general | solution.py:78
  888.6 21.4 %multiply_convert_fusion.15 = bf16[12,512,1024]{2,1,0:T(8,128)(2,1)} fusion(f32[12,512,1024]{2,1,0:T(8,128)} %get-tuple-element.815, f32[12,512]{1,0:T(8,128)S(1)} %get-tuple-element.816, f32[12,512]{1,0:T(8,128)S(1)} %dynamic-slice_bitcast_fusion.5, f32[12,512,1024]{2,1,0:T(8,128)} %fusion.247, pred[512,1024]{1,0:T(8,128)(4,1)S(1)} %fusion.248), kind=kLoop, calls=%fused_computation.66.clone.1 | loop fusion | flops 44040192 | bytes 63488000 | tf_op jit(solution)/shard_map/while/body/eval_jaxpr/while/body/eval_jaxpr/convert_element_type | solution.py:82
  921.9 27.1 %dynamic_update_slice.59 = bf16[2,512,12,64]{1,0,3,2:T(2,128)(2,1)} dynamic-update-slice(bf16[2,512,12,64]{1,0,3,2:T(2,128)(2,1)} %get-tuple-element.956, bf16[1,512,12,64]{1,0,3,2:T(2,128)(2,1)S(1)} %copy.154, s32[]{:T(128)} %get-tuple-element.953, s32[]{:T(128)} %constant.193.clone.1..sunk.3, s32[]{:T(128)} %constant.193.clone.1..sunk.3, s32[]{:T(128)} %constant.193.clone.1..sunk.3) | dynamic-update-slice | bytes 1572868 | tf_op jit(solution)/shard_map/while/body/eval_jaxpr/while/body/jit(dynamic_update_index_in_dim)/dynamic_update_slice | solution.py:60
  958.8 14.8 %bitcast_add_fusion.14 = f32[1024,12,64]{0,2,1:T(8,128)} fusion(f32[1024,12,64]{0,2,1:T(8,128)} %get-tuple-element.955, f32[12,512]{1,0:T(8,128)S(1)} %dynamic-slice_bitcast_fusion.5, f32[12,512,1024]{2,1,0:T(8,128)} %fusion.247, pred[512,1024]{1,0:T(8,128)(4,1)S(1)} %copy-done.15, pred[]{:T(512)S(6)} %compare.7, ...), kind=kOutput, calls=%fused_computation.71.clone.1 | convolution fusion | flops 838336512 | bytes 32800772 | tf_op jit(solution)/shard_map/while/body/eval_jaxpr/while/body/eval_jaxpr/hqk,qhe->khe/dot_general | solution.py:92
  1004.0 14.0 %convolution_add_fusion.1 = f32[3072,768]{1,0:T(8,128)} fusion(f32[3072,768]{1,0:T(8,128)S(1)} %fusion.99, f32[1,1024,768]{1,2,0:T(8,128)S(1)} %copy-done.25, f32[1024]{0:T(1024)S(1)} %copy-done.55, f32[1024,3072]{1,0:T(8,128)} %fusion.120), kind=kOutput, calls=%fused_computation.119 | convolution fusion | flops 4864081920 | bytes 34607104 | tf_op jit(solution)/shard_map/rsa,rsb->ab/dot_general | solution.py:26
  1028.8 13.3 convolution_add_fusion.2
  1081.8 41.1 %all-reduce.3 = (f32[2,768]{1,0:T(2,128)S(1)}, f32[2,768]{1,0:T(2,128)S(1)}, f32[5,768]{1,0:T(8,128)S(1)}) all-reduce(f32[2,768]{1,0:T(2,128)S(1)} %maximum_add_fusion, f32[2,768]{1,0:T(2,128)S(1)} %maximum_add_fusion.1, f32[5,768]{1,0:T(8,128)S(1)} %broadcast_multiply_fusion), channel_id=12, replica_groups=mesh['dp'=4,'fsdp'=8] {'dp','fsdp'}, use_global_device_ids=true, to_apply=%region_40.41.clone | all-reduce | flops 6912 | bytes 55296
  1124.8 126.3 %reduce-scatter.14.cloned.1.call-done = f32[96,768]{1,0:T(8,128)} async-done(((f32[3072,768]{1,0:T(8,128)}), f32[96,768]{1,0:T(8,128)}) %reduce-scatter.14.cloned.1.call-update) | async-done | bytes 294928 | tf_op jit(solution)/shard_map/reduce_scatter | solution.py:267
  1251.1 142.3 %reduce-scatter.12.cloned.1.call-done = f32[768,96]{0,1:T(8,128)} async-done(((f32[768,3072]{0,1:T(8,128)}), f32[768,96]{0,1:T(8,128)}) %reduce-scatter.12.cloned.1.call-update) | async-done | bytes 294928 | tf_op jit(solution)/shard_map/reduce_scatter | solution.py:266
  (490 shorter events, 526.8 us)
Async XLA Ops:
  7.2 132.7 %all-gather.8.cloned.1.call-start = ((), (), s32[]{:S(2)}) async-start(), calls=%async_computation.4 | async-start | bytes 3649536 | tf_op jit(solution)/shard_map/all_gather | solution.py:208
  7.9 232.2 %all-gather.10.cloned.1.call-start = ((), (), s32[]{:S(2)}) async-start(), calls=%async_computation.5 | async-start | bytes 1216512 | tf_op jit(solution)/shard_map/all_gather | solution.py:209
  8.7 236.0 %all-gather.12.cloned.1.call-start = ((), (), s32[]{:S(2)}) async-start(), calls=%async_computation.6 | async-start | bytes 4866048 | tf_op jit(solution)/shard_map/all_gather | solution.py:210
  9.4 252.0 %all-gather.14.cloned.1.call-start = ((), (), s32[]{:S(2)}) async-start(), calls=%async_computation.7 | async-start | bytes 4866048 | tf_op jit(solution)/shard_map/all_gather | solution.py:211
  10.0 1114.8 %reduce-scatter.10.cloned.1.call-start = ((), (), s32[]{:S(2)}) async-start(), calls=%async_computation.9 | async-start | bytes 2433024 | tf_op jit(solution)/shard_map/reduce_scatter | solution.py:265
  10.1 47.0 %copy-start.113 = (bf16[2,24]{1,0:T(2,128)(2,1)S(1)}, bf16[2,24]{1,0:T(2,128)(2,1)}, u32[]{:S(2)}) copy-start(bf16[2,24]{1,0:T(2,128)(2,1)} %param.29) | copy-start | bytes 292
  10.1 84.3 %copy-start.100 = (s32[2,1,1024]{2,1,0:T(1,128)S(1)}, s32[2,1,1024]{2,1,0:T(1,128)}, u32[]{:S(2)}) copy-start(s32[2,1,1024]{2,1,0:T(1,128)} %param.22) | copy-start | bytes 24580
  10.1 85.7 %copy-start.111 = (bf16[5,24]{1,0:T(8,128)(2,1)S(1)}, bf16[5,24]{1,0:T(8,128)(2,1)}, u32[]{:S(2)}) copy-start(bf16[5,24]{1,0:T(8,128)(2,1)} %param.30) | copy-start | bytes 724
  11.8 128.0 %copy-start.9 = (bf16[1,1024,768]{1,2,0:T(8,128)(2,1)}, bf16[1,1024,768]{1,2,0:T(8,128)(2,1)S(1)}, u32[]{:S(2)}) copy-start(bf16[1,1024,768]{1,2,0:T(8,128)(2,1)S(1)} %copy.88) | copy-start | bytes 4718596
  12.1 127.7 %copy-start.69 = (f32[1024]{0:T(1024)}, f32[1024]{0:T(1024)S(1)}, u32[]{:S(2)}) copy-start(f32[1024]{0:T(1024)S(1)} %broadcast_multiply_fusion.4) | copy-start | bytes 12292
  13.2 126.7 %copy-start.79 = (f32[1024]{0:T(1024)}, f32[1024]{0:T(1024)S(1)}, u32[]{:S(2)}) copy-start(f32[1024]{0:T(1024)S(1)} %fusion.110) | copy-start | bytes 12292
  57.1 82.8 %copy-start.58 = (f32[768]{0:T(1024)}, f32[768]{0:T(1024)S(1)}, u32[]{:S(2)}) copy-start(f32[768]{0:T(1024)S(1)} %get-tuple-element.449) | copy-start | bytes 9220
  94.4 45.5 %copy-start.104 = (f32[768]{0:T(1024)}, f32[768]{0:T(1024)S(1)}, u32[]{:S(2)}) copy-start(f32[768]{0:T(1024)S(1)} %get-tuple-element.451) | copy-start | bytes 9220
  162.2 23.6 %copy-start.44 = (bf16[1024,12,64]{0,2,1:T(8,128)(2,1)S(1)}, bf16[1024,12,64]{0,2,1:T(8,128)(2,1)}, u32[]{:S(2)}) copy-start(bf16[1024,12,64]{0,2,1:T(8,128)(2,1)} %get-tuple-element.848) | copy-start | bytes 4718596 | tf_op jit(solution)/shard_map/while/body/eval_jaxpr/while
  172.7 16.2 %copy-start = (f32[12,512,1024]{2,1,0:T(8,128)S(1)}, f32[12,512,1024]{2,1,0:T(8,128)}, u32[]{:S(2)}) copy-start(f32[12,512,1024]{2,1,0:T(8,128)} %get-tuple-element.779) | copy-start | bytes 75497472 | tf_op jit(solution)/shard_map/while/body/eval_jaxpr/while
  199.4 23.1 %copy-start.44 = (bf16[1024,12,64]{0,2,1:T(8,128)(2,1)S(1)}, bf16[1024,12,64]{0,2,1:T(8,128)(2,1)}, u32[]{:S(2)}) copy-start(bf16[1024,12,64]{0,2,1:T(8,128)(2,1)} %get-tuple-element.848) | copy-start | bytes 4718596 | tf_op jit(solution)/shard_map/while/body/eval_jaxpr/while
  210.1 15.6 %copy-start = (f32[12,512,1024]{2,1,0:T(8,128)S(1)}, f32[12,512,1024]{2,1,0:T(8,128)}, u32[]{:S(2)}) copy-start(f32[12,512,1024]{2,1,0:T(8,128)} %get-tuple-element.779) | copy-start | bytes 75497472 | tf_op jit(solution)/shard_map/while/body/eval_jaxpr/while
  234.3 27.1 %copy-start.56 = (f32[1024]{0:T(1024)}, f32[1024]{0:T(1024)S(1)}, u32[]{:S(2)}) copy-start(f32[1024]{0:T(1024)S(1)} %get-tuple-element.1009) | copy-start | bytes 12292
  244.1 17.3 %copy-start.26 = (f32[1,1024,768]{1,2,0:T(8,128)}, f32[1,1024,768]{1,2,0:T(8,128)S(1)}, u32[]{:S(2)}) copy-start(f32[1,1024,768]{1,2,0:T(8,128)S(1)} %get-tuple-element.554) | copy-start | bytes 9437188
  244.9 16.5 %copy-start.110 = (f32[768]{0:T(1024)S(1)}, f32[768]{0:T(1024)}, u32[]{:S(2)}) copy-start(f32[768]{0:T(1024)} %convolution_reduce_fusion) | copy-start | bytes 9220
  295.3 23.0 %copy-start.45 = (bf16[1024,12,64]{0,2,1:T(8,128)(2,1)S(1)}, bf16[1024,12,64]{0,2,1:T(8,128)(2,1)}, u32[]{:S(2)}) copy-start(bf16[1024,12,64]{0,2,1:T(8,128)(2,1)} %get-tuple-element.884) | copy-start | bytes 4718596 | tf_op jit(solution)/shard_map/while/body/eval_jaxpr/while
  331.8 23.0 %copy-start.45 = (bf16[1024,12,64]{0,2,1:T(8,128)(2,1)S(1)}, bf16[1024,12,64]{0,2,1:T(8,128)(2,1)}, u32[]{:S(2)}) copy-start(bf16[1024,12,64]{0,2,1:T(8,128)(2,1)} %get-tuple-element.884) | copy-start | bytes 4718596 | tf_op jit(solution)/shard_map/while/body/eval_jaxpr/while
  371.7 44.8 %copy-start.77 = (f32[1024]{0:T(1024)}, f32[1024]{0:T(1024)S(1)}, u32[]{:S(2)}) copy-start(f32[1024]{0:T(1024)S(1)} %broadcast_multiply_fusion.1) | copy-start | bytes 12292
  374.2 42.3 %copy-start.92 = (f32[1024]{0:T(1024)}, f32[1024]{0:T(1024)S(1)}, u32[]{:S(2)}) copy-start(f32[1024]{0:T(1024)S(1)} %fusion.113) | copy-start | bytes 12292
  439.6 19.1 %copy-start.12 = (pred[512,1024]{1,0:T(8,128)(4,1)}, pred[512,1024]{1,0:T(8,128)(4,1)S(1)}, u32[]{:S(2)}) copy-start(pred[512,1024]{1,0:T(8,128)(4,1)S(1)} %fusion.237) | copy-start | bytes 1572868 | tf_op jit(solution)/shard_map/while/body/eval_jaxpr/while
  556.1 19.2 %copy-start.12 = (pred[512,1024]{1,0:T(8,128)(4,1)}, pred[512,1024]{1,0:T(8,128)(4,1)S(1)}, u32[]{:S(2)}) copy-start(pred[512,1024]{1,0:T(8,128)(4,1)S(1)} %fusion.237) | copy-start | bytes 1572868 | tf_op jit(solution)/shard_map/while/body/eval_jaxpr/while
  686.0 16.0 %copy-start.37 = (f32[1,1024,768]{1,2,0:T(8,128)}, f32[1,1024,768]{1,2,0:T(8,128)S(1)}, u32[]{:S(2)}) copy-start(f32[1,1024,768]{1,2,0:T(8,128)S(1)} %get-tuple-element.532) | copy-start | bytes 9437188
  729.4 395.3 %reduce-scatter.8.cloned.1.call-start = ((), (), s32[]{:S(2)}) async-start(), calls=%async_computation.8 | async-start | bytes 7299072 | tf_op jit(solution)/shard_map/reduce_scatter | solution.py:264
  751.3 19.4 %copy-start.14 = (pred[512,1024]{1,0:T(8,128)(4,1)}, pred[512,1024]{1,0:T(8,128)(4,1)S(1)}, u32[]{:S(2)}) copy-start(pred[512,1024]{1,0:T(8,128)(4,1)S(1)} %fusion.248) | copy-start | bytes 1572868 | tf_op jit(solution)/shard_map/while/body/eval_jaxpr/while
  869.3 19.2 %copy-start.14 = (pred[512,1024]{1,0:T(8,128)(4,1)}, pred[512,1024]{1,0:T(8,128)(4,1)S(1)}, u32[]{:S(2)}) copy-start(pred[512,1024]{1,0:T(8,128)(4,1)S(1)} %fusion.248) | copy-start | bytes 1572868 | tf_op jit(solution)/shard_map/while/body/eval_jaxpr/while
  991.6 259.5 %reduce-scatter.14.cloned.1.call-start = ((), (), s32[]{:S(2)}) async-start(), calls=%async_computation.11 | async-start | bytes 9732096 | tf_op jit(solution)/shard_map/reduce_scatter | solution.py:267
  1018.1 375.3 %reduce-scatter.12.cloned.1.call-start = ((), (), s32[]{:S(2)}) async-start(), calls=%async_computation.10 | async-start | bytes 9732096 | tf_op jit(solution)/shard_map/reduce_scatter | solution.py:266
  (117 other events, 602.8 us)
Sparse Core Ops, SparseCore 0:
  11.0 63.1 all-gather.7
  77.2 53.0 all-gather.9
  133.3 62.5 all-gather.11
  198.8 62.5 all-gather.13
  729.5 97.7 reduce-scatter.9
  991.7 118.1 reduce-scatter.7
  1116.4 134.6 reduce-scatter.13
  1258.6 134.8 reduce-scatter.11
where the time goes:
time: 1420 us; the launch traced here: 1400 us
  matrix products  531 us (37%)
  waiting for transfers between devices  277 us (20%)
  local copies, waits for them, and re-layouts  227 us (16%)
  other arithmetic  175 us (12%)
  blocking collectives  159 us (11%)
  between operations  17.2 us (1%)
  loops' own time  14.9 us (1%)
    reduce_scatter x1, waiting for transfers between devices, body(): lax.psum_scatter(grads_first[2], ('dp', 'fsdp'), scatter_dimension=1, til...  142 us
    reduce_scatter x1, waiting for transfers between devices, body(): lax.psum_scatter(grads_first[3], ('dp', 'fsdp'), scatter_dimension=0, til...  126 us
    dynamic_update_slice x8, local copies, waits for them, and re-layouts, attend_forward(): lax.map(one_block, jnp.arange(seq_length // block_rows, dtype=jnp.int32))  119 us
    convert_element_type x4, other arithmetic, one_block(): score_grad = (soft * (soft_grad - row_dot)).astype(jnp.bfloat16)  85.8 us
    dot_general x8, matrix products, block_scores(): jnp.einsum('qhe,khe->hqk', query_rows, key_heads, preferred_element_type=...  85.7 us
    dot_general x4, matrix products, one_block(): jnp.einsum('qhe,khe->hqk', grad_rows, value_heads, preferred_element_type...  76.8 us
    dot_general x8, matrix products, weight_grad(): jnp.einsum('rsa,rsb->ab', left_side, right_side, preferred_element_type=j...  63 us
    dot_general x4, matrix products, one_block(): jnp.einsum('hqk,qhe->khe', soft_low, grad_rows, preferred_element_type=jn...  57.5 us
  transfers between devices with their start and end apart: 8, of which 3 were waited for; matrix products, arithmetic and copies ran while one was open for 33% of the time, Pallas kernels for 0%

commit v1 on v0

v1 whole, which is shorter than its diff:
```python
import functools

import jax
import jax.numpy as jnp
from jax import lax
from jax.experimental import pallas as pl
from jax.experimental.pallas import tpu as pltpu
from jax.sharding import PartitionSpec as P

HEAD = 64
LANES = 128
AXES = ("dp", "fsdp")
bf16 = jnp.bfloat16
f32 = jnp.float32

norm_epsilon = 1e-05
masked_score = -1000000000.0
curve_one = 0.7978845608028654
curve_three = 0.7978845608028654 * 0.044715

VMEM_LIMIT = 60 * 1024 * 1024


def dot_nn(left, right):
    return lax.dot_general(left, right, (((1,), (0,)), ((), ())), preferred_element_type=f32)


def dot_nt(left, right):
    return lax.dot_general(left, right, (((1,), (1,)), ((), ())), preferred_element_type=f32)


def dot_tn(left, right):
    return lax.dot_general(left, right, (((0,), (0,)), ((), ())), preferred_element_type=f32)


def normalize(values):
    center = jnp.mean(values, axis=-1, keepdims=True)
    centered = values - center
    spread = jnp.mean(centered * centered, axis=-1, keepdims=True)
    scale = lax.rsqrt(spread + norm_epsilon)
    return centered * scale, scale


def norm_back(grad, gain, xhat, scale):
    gained = grad * gain
    first = jnp.mean(gained, axis=-1, keepdims=True)
    second = jnp.mean(gained * xhat, axis=-1, keepdims=True)
    return scale * (gained - first - xhat * second)


def gelu_pair(lifted):
    square = lifted * lifted
    cubic = curve_three * square
    half = 0.5 + 0.5 * jnp.tanh(lifted * (curve_one + cubic))
    value = lifted * half
    slope = half + value * ((1.0 - half) * (2.0 * curve_one + 6.0 * cubic))
    return value, slope


def call(kernel, grid, in_specs, out_specs, out_shape, flops, args, scratch=()):
    moved = sum(a.size * a.dtype.itemsize for a in args)
    moved += sum(o.size * o.dtype.itemsize for o in out_shape)
    return pl.pallas_call(
        kernel,
        grid=grid,
        in_specs=in_specs,
        out_specs=out_specs,
        out_shape=out_shape,
        scratch_shapes=list(scratch),
        compiler_params=pltpu.CompilerParams(
            dimension_semantics=("arbitrary",) * len(grid), vmem_limit_bytes=VMEM_LIMIT
        ),
        cost_estimate=pl.CostEstimate(flops=flops, bytes_accessed=moved, transcendentals=0),
    )(*args)


def rows_spec(block_rows, width):
    return pl.BlockSpec((block_rows, width), lambda i: (i, 0))


def whole_spec(array):
    zeros = (0,) * len(array.shape)
    return pl.BlockSpec(array.shape, lambda i: zeros, pipeline_mode=pl.Buffered(1))


def sds(shape, dtype):
    return jax.ShapeDtypeStruct(shape, dtype)


def head_part(x, gain, shift, w_qkv, mixed_ref, normed_ref):
    xhat, _ = normalize(x)
    normed = (xhat * gain + shift).astype(bf16)
    normed_ref[...] = normed
    mixed_ref[...] = dot_nt(normed, w_qkv[...]).astype(bf16)


def first_kernel(x_ref, norms_ref, wq_ref, mixed_ref, normed_ref):
    head_part(
        x_ref[...].astype(f32), norms_ref[0:1, :], norms_ref[2:3, :], wq_ref, mixed_ref, normed_ref
    )


def ff_chunks(ff):
    step = 768 if ff % 768 == 0 else ff
    return [pl.ds(at, step) for at in range(0, ff, step)]


def middle_kernel(
    att_ref, x_ref, live_ref, norms_ref, emb_ref, wo_ref, wu_ref, wd_ref, wq_ref,
    hidden_ref, second_ref, act_ref, slope_ref, later_ref, mixed_ref, normed_ref,
):
    live = live_ref[...]
    hidden = x_ref[...].astype(f32) + live * dot_nt(att_ref[...], wo_ref[...])
    hidden_ref[...] = hidden
    xhat, _ = normalize(hidden)
    second = (xhat * norms_ref[1:2, :] + norms_ref[3:4, :]).astype(bf16)
    second_ref[...] = second
    total = jnp.zeros_like(hidden)
    for part in ff_chunks(wu_ref.shape[0]):
        value, slope = gelu_pair(dot_nt(second, wu_ref[part, :]))
        value = value.astype(bf16)
        act_ref[:, part] = value
        slope_ref[:, part] = slope.astype(bf16)
        total = total + dot_nn(value, wd_ref[part, :])
    later = hidden + live * total + emb_ref[...]
    later_ref[...] = later
    head_part(later, norms_ref[0:1, :], norms_ref[2:3, :], wq_ref, mixed_ref, normed_ref)


def mlp_back_tail(
    grad, live, hidden, second_grad, norms_ref, wo_ref, branch_ref, hgrad_ref, agrad_ref
):
    xhat, scale = normalize(hidden)
    hgrad = grad + norm_back(second_grad, norms_ref[1:2, :], xhat, scale)
    hgrad_ref[...] = hgrad
    branch = (live * hgrad).astype(bf16)
    branch_ref[...] = branch
    agrad_ref[...] = dot_nn(branch, wo_ref[...]).astype(bf16)
    gain_sum = jnp.sum(second_grad * xhat, axis=0, keepdims=True)
    shift_sum = jnp.sum(second_grad, axis=0, keepdims=True)
    return gain_sum, shift_sum


def add_sums(sums_ref, sums):
    @pl.when(pl.program_id(0) == 0)
    def _():
        sums_ref[...] = jnp.zeros_like(sums_ref)

    for place, value in enumerate(sums):
        sums_ref[place : place + 1, :] += value


def turn_kernel(
    att_ref, x_ref, live_ref, norms_ref, grad_ref, wo_ref, wu_ref, wd_ref,
    out_ref, second_ref, act_ref, drop_ref, lift_ref, branch_ref, hgrad_ref, agrad_ref, sums_ref,
):
    live = live_ref[...]
    hidden = x_ref[...] + live * dot_nt(att_ref[...], wo_ref[...])
    xhat, _ = normalize(hidden)
    second = (xhat * norms_ref[1:2, :] + norms_ref[3:4, :]).astype(bf16)
    second_ref[...] = second
    grad = grad_ref[...]
    drop = (live * grad).astype(bf16)
    drop_ref[...] = drop
    total = jnp.zeros_like(hidden)
    second_grad = jnp.zeros_like(hidden)
    for part in ff_chunks(wu_ref.shape[0]):
        value, slope = gelu_pair(dot_nt(second, wu_ref[part, :]))
        value = value.astype(bf16)
        act_ref[:, part] = value
        total = total + dot_nn(value, wd_ref[part, :])
        lift = (dot_nt(drop, wd_ref[part, :]) * slope).astype(bf16)
        lift_ref[:, part] = lift
        second_grad = second_grad + dot_nn(lift, wu_ref[part, :])
    out_ref[...] = (hidden + live * total).astype(bf16)
    sums = mlp_back_tail(
        grad, live, hidden, second_grad, norms_ref, wo_ref, branch_ref, hgrad_ref, agrad_ref
    )
    add_sums(sums_ref, sums)


def head_back(mixed_grad_ref, wq_ref, x, hgrad, norms_ref):
    width = x.shape[1]
    normed_grad = dot_nn(mixed_grad_ref[0], wq_ref[0:width, :])
    normed_grad += dot_nn(mixed_grad_ref[1], wq_ref[width : 2 * width, :])
    normed_grad += dot_nn(mixed_grad_ref[2], wq_ref[2 * width : 3 * width, :])
    xhat, scale = normalize(x)
    grad = hgrad + norm_back(normed_grad, norms_ref[0:1, :], xhat, scale)
    gain_sum = jnp.sum(normed_grad * xhat, axis=0, keepdims=True)
    shift_sum = jnp.sum(normed_grad, axis=0, keepdims=True)
    return grad, gain_sum, shift_sum


def back_kernel(
    mgrad_ref, later_ref, hgrad1_ref, norms_ref, live_ref, hidden_ref, slope_ref,
    wq_ref, wo_ref, wu_ref, wd_ref,
    drop_ref, lift_ref, branch_ref, hgrad_ref, agrad_ref, sums_ref,
):
    grad, gain0, shift0 = head_back(mgrad_ref, wq_ref, later_ref[...], hgrad1_ref[...], norms_ref)
    table_sum = jnp.sum(grad, axis=0, keepdims=True)
    live = live_ref[...]
    drop = (live * grad).astype(bf16)
    drop_ref[...] = drop
    second_grad = jnp.zeros_like(grad)
    for part in ff_chunks(wu_ref.shape[0]):
        lift = (dot_nt(drop, wd_ref[part, :]) * slope_ref[:, part].astype(f32)).astype(bf16)
        lift_ref[:, part] = lift
        second_grad = second_grad + dot_nn(lift, wu_ref[part, :])
    sums = mlp_back_tail(
        grad, live, hidden_ref[...], second_grad, norms_ref, wo_ref, branch_ref, hgrad_ref, agrad_ref
    )
    add_sums(sums_ref, sums + (gain0, shift0, table_sum))


def last_kernel(mgrad_ref, x_ref, hgrad_ref, norms_ref, wq_ref, out_ref, sums_ref):
    grad, gain0, shift0 = head_back(
        mgrad_ref, wq_ref, x_ref[...].astype(f32), hgrad_ref[...], norms_ref
    )
    out_ref[...] = grad
    add_sums(sums_ref, (gain0, shift0))


def ff_grad_kernel(
    act0, act1, lift0, lift1, drop0, drop1, second0, second1, up_ref, down_ref
):
    down_ref[...] = (dot_tn(act0[...], drop0[...]) + dot_tn(act1[...], drop1[...])).astype(bf16)
    up_ref[...] = (dot_tn(lift0[...], second0[...]) + dot_tn(lift1[...], second1[...])).astype(bf16)


def pair_grad_kernel(left0, left1, right0, right1, out_ref):
    out_ref[...] = (dot_tn(left0[...], right0[...]) + dot_tn(left1[...], right1[...])).astype(bf16)


def ff_grads(kept0, kept1):
    tokens, ff = kept0["act"].shape
    width = kept0["drop"].shape[1]
    step = 384
    cols = pl.BlockSpec((tokens, step), lambda i: (0, i))
    full = [kept0["drop"], kept1["drop"], kept0["second"], kept1["second"]]
    args = [kept0["act"], kept1["act"], kept0["lift"], kept1["lift"]] + full
    return call(
        ff_grad_kernel,
        (ff // step,),
        [cols] * 4 + [whole_spec(a) for a in full],
        [rows_spec(step, width)] * 2,
        [sds((ff, width), bf16)] * 2,
        8 * tokens * ff * width,
        args,
    )


def pair_grads(left0, left1, right0, right1, step):
    tokens, high = left0.shape
    width = right0.shape[1]
    cols = pl.BlockSpec((tokens, step), lambda i: (0, i))
    return call(
        pair_grad_kernel,
        (high // step,),
        [cols] * 2 + [whole_spec(right0)] * 2,
        [rows_spec(step, width)],
        [sds((high, width), bf16)],
        4 * tokens * high * width,
        [left0, left1, right0, right1],
    )[0]


def qkv_grad_kernel(left0, left1, right0, right1, out_ref):
    out_ref[...] = (dot_tn(left0[0], right0[...]) + dot_tn(left1[0], right1[...])).astype(bf16)


def qkv_grads(left0, left1, right0, right1, step=384):
    parts, tokens, high = left0.shape
    width = right0.shape[1]
    per = high // step
    cols = pl.BlockSpec((1, tokens, step), lambda i: (i // per, 0, i % per))
    return call(
        qkv_grad_kernel,
        (parts * per,),
        [cols] * 2 + [whole_spec(right0)] * 2,
        [rows_spec(step, width)],
        [sds((parts * high, width), bf16)],
        4 * tokens * parts * high * width,
        [left0, left1, right0, right1],
    )[0]


def lane_index(shape):
    return lax.broadcasted_iota(jnp.int32, shape, len(shape) - 1)


def split_three(values):
    high = values.astype(bf16)
    rest = values - high.astype(f32)
    middle = rest.astype(bf16)
    low = (rest - middle.astype(f32)).astype(bf16)
    return high, middle, low


def own_lanes(lane, head):
    return (lane < HEAD) if head == 0 else (lane >= HEAD)


def attend_kernel(
    block, q_ref, k_ref, v_ref, live_col_ref, live_row_ref, out_ref, logs_ref, mask_ref
):
    seq = q_ref.shape[0]
    count = seq // block

    @pl.when(pl.program_id(0) == 0)
    def _():
        query = lax.broadcasted_iota(jnp.int32, (block, block), 0)
        key = lax.broadcasted_iota(jnp.int32, (block, block), 1)
        for i in range(count):
            alive = live_row_ref[:, i * block : (i + 1) * block] > 0.5
            visible = (key <= query) & (alive | (key == query))
            mask_ref[i] = jnp.where(visible, 0.0, masked_score)

    lane = lane_index((seq, LANES))
    q = q_ref[...] * 0.125
    k = k_ref[...]
    v = v_ref[...]
    bias = ((live_col_ref[...] - 1.0) * 1e9).astype(bf16)
    zero = jnp.zeros((seq, LANES), bf16)
    one = jnp.ones((seq, LANES), bf16)
    parts = []
    for head in range(2):
        mine = own_lanes(lane, head)
        spare = (1 - head) * HEAD
        parts.append(
            (
                jnp.where(mine, q, zero),
                jnp.where(mine, q, jnp.where(lane == spare, one, zero)),
                jnp.where(mine, k, jnp.where(lane == spare, bias, zero)),
                jnp.where(mine, v, one),
            )
        )
    low = lane_index((block, LANES)) < HEAD
    for i in range(count):
        at = slice(i * block, (i + 1) * block)
        before = slice(0, i * block)
        outs, logs = [], []
        for head in range(2):
            q_plain, q_bias, k_bias, v_ones = parts[head]
            diag = dot_nt(q_plain[at], k[at]) + mask_ref[i]
            top = jnp.max(diag, axis=-1, keepdims=True)
            if i > 0:
                off = dot_nt(q_bias[at], k_bias[before])
                top = jnp.maximum(top, jnp.max(off, axis=-1, keepdims=True))
            total = dot_nn(jnp.exp(diag - top).astype(bf16), v_ones[at])
            if i > 0:
                total += dot_nn(jnp.exp(off - top).astype(bf16), v_ones[before])
            spare = (1 - head) * HEAD
            weight = total[:, spare : spare + 1]
            outs.append(total * (1.0 / weight))
            logs.append(top + jnp.log(weight))
        out_ref[at, :] = jnp.where(low, outs[0], outs[1]).astype(bf16)
        logs_ref[at, :] = jnp.where(low, logs[0], logs[1])


def attend(mixed, live_col, live_row, block=256):
    seq, triple = mixed.shape
    width = triple // 3
    pairs = width // LANES
    block = min(block, seq)

    def cols(offset):
        return pl.BlockSpec((seq, LANES), lambda h: (0, offset + h))

    return call(
        functools.partial(attend_kernel, block),
        (pairs,),
        [cols(0), cols(pairs), cols(2 * pairs), whole_spec(live_col), whole_spec(live_row)],
        [cols(0), cols(0)],
        [sds((seq, width), bf16), sds((seq, width), f32)],
        4 * seq * seq * width,
        [mixed, mixed, mixed, live_col, live_row],
        scratch=[pltpu.VMEM((seq // block, block, block), f32)],
    )


def attend_back_kernel(
    block, q_ref, k_ref, v_ref, grad_ref, att_ref, logs_ref, live_col_ref, out_ref,
    mask_ref, dk_ref, dv_ref,
):
    seq = q_ref.shape[0]
    count = seq // block

    @pl.when(pl.program_id(0) == 0)
    def _():
        key = lax.broadcasted_iota(jnp.int32, (block, block), 0)
        query = lax.broadcasted_iota(jnp.int32, (block, block), 1)
        for i in range(count):
            alive = live_col_ref[i * block : (i + 1) * block, :] > 0.5
            visible = (key <= query) & (alive | (key == query))
            mask_ref[i] = jnp.where(visible, 0.0, masked_score)

    lane = lane_index((seq, LANES))
    q = q_ref[...] * 0.125
    k = k_ref[...]
    v = v_ref[...]
    grad = grad_ref[...]
    logs = logs_ref[...]
    dots = grad.astype(f32) * att_ref[...].astype(f32)
    bias = ((live_col_ref[...] - 1.0) * 1e9).astype(bf16)
    zero = jnp.zeros((seq, LANES), bf16)
    one = jnp.ones((seq, LANES), bf16)
    parts = []
    for head in range(2):
        mine = own_lanes(lane, head)
        spare = (1 - head) * HEAD
        log_terms = split_three(-logs[:, head * HEAD : head * HEAD + 1])
        dot_terms = split_three(-jnp.sum(jnp.where(mine, dots, 0.0), axis=-1, keepdims=True))
        q_more, k_more, k_diag, g_more, v_more = (
            jnp.where(lane == spare, one, zero),
            jnp.where(lane == spare, bias, zero),
            zero,
            zero,
            zero,
        )
        for place in range(3):
            here = lane == spare + 1 + place
            q_more = jnp.where(here, log_terms[place], q_more)
            k_more = jnp.where(here, one, k_more)
            k_diag = jnp.where(here, one, k_diag)
            g_more = jnp.where(here, dot_terms[place], g_more)
            v_more = jnp.where(here, one, v_more)
        parts.append(
            dict(
                q=jnp.where(mine, q, q_more),
                k=jnp.where(mine, k, k_more),
                kd=jnp.where(mine, k, k_diag),
                g=jnp.where(mine, grad, g_more),
                v=jnp.where(mine, v, v_more),
                q0=jnp.where(mine, q, zero),
                k0=jnp.where(mine, k, zero),
                g0=jnp.where(mine, grad, zero),
            )
        )
    for i in range(count):
        at = slice(i * block, (i + 1) * block)
        dq = jnp.zeros((block, LANES), f32)
        for j in range(i + 1):
            to = slice(j * block, (j + 1) * block)
            dk = jnp.zeros((block, LANES), f32)
            dv = jnp.zeros((block, LANES), f32)
            for head in range(2):
                part = parts[head]
                if j == i:
                    score = dot_nt(part["kd"][to], part["q"][at]) + mask_ref[i]
                else:
                    score = dot_nt(part["k"][to], part["q"][at])
                soft = jnp.exp(score)
                change = (soft * dot_nt(part["v"][to], part["g"][at])).astype(bf16)
                dv += dot_nn(soft.astype(bf16), part["g0"][at])
                dk += dot_nn(change, part["q0"][at])
                dq += dot_tn(change, part["k0"][to])
            if j == i:
                dk_ref[to, :] = dk
                dv_ref[to, :] = dv
            else:
                dk_ref[to, :] += dk
                dv_ref[to, :] += dv
        out_ref[0, at, :] = (dq * 0.125).astype(bf16)
    out_ref[1] = dk_ref[...].astype(bf16)
    out_ref[2] = dv_ref[...].astype(bf16)


def attend_back(mixed, att_grad, att, logs, live_col, block=256):
    seq, triple = mixed.shape
    width = triple // 3
    pairs = width // LANES
    block = min(block, seq)

    def cols(offset):
        return pl.BlockSpec((seq, LANES), lambda h: (0, offset + h))

    return call(
        functools.partial(attend_back_kernel, block),
        (pairs,),
        [cols(0), cols(pairs), cols(2 * pairs), cols(0), cols(0), cols(0), whole_spec(live_col)],
        [pl.BlockSpec((3, seq, LANES), lambda h: (0, 0, h))],
        [sds((3, seq, width), bf16)],
        10 * seq * seq * width,
        [mixed, mixed, mixed, att_grad, att, logs, live_col],
        scratch=[
            pltpu.VMEM((seq // block, block, block), f32),
            pltpu.VMEM((seq, LANES), f32),
            pltpu.VMEM((seq, LANES), f32),
        ],
    )[0]


def gather_all(w_qkv, w_out, w_up, w_down, norm_gains, norm_shifts, pass_table):
    width = w_out.shape[0]
    small = jnp.concatenate([norm_gains, norm_shifts, pass_table], axis=0)
    count, share = small.shape
    rows = [w_qkv.shape[1], w_out.shape[1], w_up.shape[1], w_down.shape[0]]
    flat = small.reshape(1, -1)
    slots = -(-flat.shape[1] // width)
    flat = jnp.pad(flat, ((0, 0), (0, slots * width - flat.shape[1]))).reshape(slots, width)
    packed = jnp.concatenate([w_qkv.T, w_out.T, w_up.T, w_down, flat], axis=0)
    fill = -packed.shape[0] % 16
    packed = jnp.pad(packed, ((0, fill), (0, 0)))
    whole = lax.all_gather(packed, AXES, axis=0, tiled=False)
    devices = whole.shape[0]
    found, at = [], 0
    for size in rows:
        found.append(whole[:, at : at + size].reshape(devices * size, width))
        at += size
    small = whole[:, at : at + slots].reshape(devices, slots * width)[:, : count * share]
    small = small.reshape(devices, count, share).transpose(1, 0, 2).reshape(count, devices * share)
    return tuple(found), small.astype(f32)


def body(
    tokens, row_lengths, live_mask, pass_index,
    w_qkv, w_out, w_up, w_down, norm_gains, norm_shifts, pass_table, cotangent,
):
    _, seq, width = tokens.shape
    ff = w_up.shape[1] * lax.axis_size(AXES)
    block = min(256, seq)
    grid = (seq // block,)
    passes = pass_table.shape[0]

    (wq, wo, wu, wd), small = gather_all(
        w_qkv, w_out, w_up, w_down, norm_gains, norm_shifts, pass_table
    )
    norms = jnp.concatenate([small[:4], jnp.zeros((4, width), f32)], axis=0)
    chosen = jnp.where(jnp.arange(passes, dtype=jnp.int32) == pass_index[0], 1.0, 0.0).astype(f32)
    emb = jnp.sum(chosen[:, None] * small[4:], axis=0, keepdims=True)

    positions = jnp.arange(seq, dtype=jnp.int32)
    inside = positions < row_lengths[0]
    live = jnp.where(inside[None, :] & (live_mask[:, 0] > 0), 1.0, 0.0).astype(f32)
    live_cols = [live[0][:, None], live[1][:, None]]
    live_rows = [live[0][None, :], live[1][None, :]]

    x = tokens[0]
    given = cotangent[0]
    rows_w = rows_spec(block, width)
    rows_f = rows_spec(block, ff)
    rows_q = rows_spec(block, 3 * width)
    rows_1 = rows_spec(block, 1)
    rows_3 = pl.BlockSpec((3, block, width), lambda i: (0, i, 0))
    sums_spec = pl.BlockSpec((8, width), lambda i: (0, 0))
    wide = sds((seq, width), f32)
    thin = sds((seq, width), bf16)
    tall = sds((seq, ff), bf16)
    triple = sds((seq, 3 * width), bf16)
    sums_shape = sds((8, width), f32)
    unit = 2 * seq * width

    mixed0, normed0 = call(
        first_kernel, grid,
        [rows_w, whole_spec(norms), whole_spec(wq)],
        [rows_q, rows_w], [triple, thin], unit * 3 * width, [x, norms, wq],
    )
    att0, logs0 = attend(mixed0, live_cols[0], live_rows[0])
    hidden0, second0, act0, slope0, later, mixed1, normed1 = call(
        middle_kernel, grid,
        [rows_w, rows_w, rows_1] + [whole_spec(a) for a in (norms, emb, wo, wu, wd, wq)],
        [rows_w, rows_w, rows_f, rows_f, rows_w, rows_q, rows_w],
        [wide, thin, tall, tall, wide, triple, thin],
        unit * (4 * width + 2 * ff),
        [att0, x, live_cols[0], norms, emb, wo, wu, wd, wq],
    )
    att1, logs1 = attend(mixed1, live_cols[1], live_rows[1])
    result, second1, act1, drop1, lift1, branch1, hgrad1, agrad1, sums1 = call(
        turn_kernel, grid,
        [rows_w, rows_w, rows_1, whole_spec(norms), rows_w] + [whole_spec(a) for a in (wo, wu, wd)],
        [rows_w, rows_w, rows_f, rows_w, rows_f, rows_w, rows_w, rows_w, sums_spec],
        [thin, thin, tall, thin, tall, thin, wide, thin, sums_shape],
        unit * (2 * width + 4 * ff),
        [att1, later, live_cols[1], norms, given, wo, wu, wd],
    )
    mgrad1 = attend_back(mixed1, agrad1, att1, logs1, live_cols[1])
    drop0, lift0, branch0, hgrad0, agrad0, sums0 = call(
        back_kernel, grid,
        [rows_3, rows_w, rows_w, whole_spec(norms), rows_1, rows_w, rows_f]
        + [whole_spec(a) for a in (wq, wo, wu, wd)],
        [rows_w, rows_f, rows_w, rows_w, rows_w, sums_spec],
        [thin, tall, thin, wide, thin, sums_shape],
        unit * (4 * width + 2 * ff),
        [mgrad1, later, hgrad1, norms, live_cols[0], hidden0, slope0, wq, wo, wu, wd],
    )
    up_grad, down_grad = ff_grads(
        dict(act=act0, lift=lift0, drop=drop0, second=second0),
        dict(act=act1, lift=lift1, drop=drop1, second=second1),
    )
    out_grad = pair_grads(branch0, branch1, att0, att1, 384)
    mgrad0 = attend_back(mixed0, agrad0, att0, logs0, live_cols[0])
    qkv_grad = qkv_grads(mgrad0, mgrad1, normed0, normed1)
    input_grad, sums_last = call(
        last_kernel, grid,
        [rows_3, rows_w, rows_w, whole_spec(norms), whole_spec(wq)],
        [rows_w, sums_spec], [wide, sums_shape], unit * 3 * width,
        [mgrad0, x, hgrad0, norms, wq],
    )

    gain0 = sums0[2] + sums_last[0]
    shift0 = sums0[3] + sums_last[1]
    gain1 = sums0[0] + sums1[0]
    shift1 = sums0[1] + sums1[1]
    table = chosen[:, None] * sums0[4][None, :]
    small_grad = jnp.concatenate([jnp.stack([gain0, gain1, shift0, shift1]), table], axis=0)

    def scatter(grads):
        return lax.psum_scatter(grads, AXES, scatter_dimension=0, tiled=True).astype(f32)

    up = scatter(up_grad).T
    down = scatter(down_grad)
    out = scatter(out_grad).T
    qkv = scatter(qkv_grad).T
    small = lax.psum_scatter(small_grad, AXES, scatter_dimension=1, tiled=True)
    return (
        result[None], input_grad[None], qkv, out, up, down,
        small[:2], small[2], small[3], small[4:],
    )


def solution(mesh):
    placed = (
        P(AXES, None, None),
        P(AXES),
        P(None, AXES, None),
        P(AXES),
        P(None, AXES),
        P(None, AXES),
        P(None, AXES),
        P(AXES, None),
        P(None, AXES),
        P(None, AXES),
        P(None, AXES),
        P(AXES, None, None),
    )
    return jax.shard_map(
        body,
        mesh=mesh,
        in_specs=placed,
        out_specs=(
            P(AXES, None, None),
            P(AXES, None, None),
            P(None, AXES),
            P(None, AXES),
            P(None, AXES),
            P(AXES, None),
            P(None, AXES),
            P(AXES),
            P(AXES),
            P(None, AXES),
        ),
        check_vma=False,
    )
```

time: 1420 us -> 775 us (0.55)
  matrix products: 531 us -> 0 us
  Pallas kernels: 0 us -> 280 us
  local copies, waits for them, and re-layouts: 227 us -> 25.6 us
  other arithmetic: 175 us -> 9.39 us
  blocking collectives: 159 us -> 38.9 us
  waiting for transfers between devices: 277 us -> 396 us
  loops' own time: 14.9 us -> 0 us
    dot_general x53 -> x0, matrix products: 531 us -> none  [the longest x8 85.7 us: block_scores(): jnp.einsum('qhe,khe->hqk', query_rows, key_heads, preferred_element_type=...]
    pallas_call x0 -> x12, Pallas kernels: none -> 280 us  [call(): pl.pallas_call(kernel, grid=grid, in_specs=in_specs, out_specs=out_specs,...]
    dynamic_update_slice x8 -> x0, local copies, waits for them, and re-layouts: 119 us -> none  [attend_forward(): lax.map(one_block, jnp.arange(seq_length // block_rows, dtype=jnp.int32))]
    all_gather x3 -> x0, blocking collectives: 118 us -> none  [the longest x1 43 us: fetch(): lax.all_gather(norm_gains, ('dp', 'fsdp'), axis=1, tiled=True)]
    all_gather x4 -> x1, waiting for transfers between devices: 5.28 us -> 105 us  [gather_all(): whole = lax.all_gather(packed, AXES, axis=0, tiled=False)]
    convert_element_type x6 -> x2, other arithmetic: 91.7 us -> 1.65 us  [the longest x1 1.64 us: scatter(): lax.psum_scatter(grads, AXES, scatter_dimension=0, tiled=True).astype(f32)]
    reduce_sum x18 -> x1, other arithmetic: 72 us -> 0.08 us  [body(): emb = jnp.sum(chosen[:, None] * small[4:], axis=0, keepdims=True)]
    unnamed x244 -> x9, local copies, waits for them, and re-layouts: 29 us -> 3.55 us
  transfers between devices with their start and end apart: 8 -> 5, of which waited for: 3 -> 4; matrix products, arithmetic and copies ran while one was open for 33% -> 1% of each run, Pallas kernels for 0% -> 11%
where the time goes in v1:
time: 775 us; the launch traced here: 766 us
  waiting for transfers between devices  396 us (51%)
  Pallas kernels  280 us (36%)
  blocking collectives  38.9 us (5%)
  local copies, waits for them, and re-layouts  25.6 us (3%)
  between operations  15.7 us (2%)
  other arithmetic  9.39 us (1%)
    reduce_scatter x4, waiting for transfers between devices, scatter(): lax.psum_scatter(grads, AXES, scatter_dimension=0, tiled=True).astype(f32)  291 us
    pallas_call x12, Pallas kernels, call(): pl.pallas_call(kernel, grid=grid, in_specs=in_specs, out_specs=out_specs,...  280 us
    all_gather x1, waiting for transfers between devices, gather_all(): whole = lax.all_gather(packed, AXES, axis=0, tiled=False)  105 us
    unnamed x1, blocking collectives  38.9 us
  transfers between devices with their start and end apart: 5, of which 4 were waited for; matrix products, arithmetic and copies ran while one was open for 1% of the time, Pallas kernels for 11%

profile of v1, /device:TPU:0, one launch (start us, length us, event | category | flops | bytes accessed | tf_op | source)
XLA Modules:
  0.0 766.4 jit_solution(16177279530562258915)
XLA Ops:
  7.2 0.9 bitcast_dynamic-update-slice_fusion.1
  9.7 0.9 bitcast_dynamic-update-slice_fusion
  10.6 0.9 constant_dynamic-update-slice_fusion.1
  11.6 0.8 pad.10
  14.4 1.1 copy.53.live_col_ref.live_ref
  16.1 1.1 copy.56.live_col_ref.live_ref
  17.2 104.7 %all-gather.3.cloned.1.call-done = bf16[9728,768]{1,0:T(8,128)(2,1)} async-done(((bf16[304,768]{1,0:T(8,128)(2,1)}), bf16[9728,768]{1,0:T(8,128)(2,1)}) %all-gather.3.cloned.1.call-update) | async-done | bytes 14942224 | tf_op jit(solution)/shard_map/all_gather | solution.py:504
  121.9 1.0 slice.100
  122.9 4.0 slice.103
  126.9 7.9 %fusion.1 = (bf16[32,96,768]{2,1,0:T(8,128)(2,1)}, bf16[32,96,768]{2,1,0:T(8,128)(2,1)}) fusion(bf16[32,304,768]{2,1,0:T(8,128)(2,1)} %bitcast.47), kind=kLoop, calls=%fused_computation.28 | loop fusion | bytes 18874368 | tf_op jit(solution)/shard_map/slice | solution.py:508
  134.9 2.4 slice.106
  139.2 8.5 %shard_map.195 = (bf16[1024,2304]{1,0:T(8,128)(2,1)}, bf16[1024,768]{1,0:T(8,128)(2,1)}) custom-call(bf16[1024,768]{1,0:T(8,128)(2,1)} %bitcast.66, f32[8,768]{1,0:T(8,128)} %broadcast_select_fusion.norms_ref, bf16[2304,768]{1,0:T(8,128)(2,1)} %bitcast.55), custom_call_target="tpu_custom_call" | custom-call | flops 3623878656 | bytes 11427840 | tf_op jit(solution)/shard_map/pallas_call | solution.py:63
  147.7 22.5 %shard_map.196 = (bf16[1024,768]{1,0:T(8,128)(2,1)}, f32[1024,768]{1,0:T(8,128)}) custom-call(bf16[1024,2304]{1,0:T(8,128)(2,1)} %get-tuple-element.42.q_ref.k_ref.v_ref, bf16[1024,2304]{1,0:T(8,128)(2,1)} %get-tuple-element.42.q_ref.k_ref.v_ref, bf16[1024,2304]{1,0:T(8,128)(2,1)} %get-tuple-element.42.q_ref.k_ref.v_ref, ...), custom_call_target="tpu_custom_call" | custom-call | flops 3221225472 | bytes 18882560 | tf_op jit(solution)/shard_map/pallas_call | solution.py:63
  170.1 28.3 %shard_map.197 = (f32[1024,768]{1,0:T(8,128)}, bf16[1024,768]{1,0:T(8,128)(2,1)}, bf16[1024,3072]{1,0:T(8,128)(2,1)}, bf16[1024,3072]{1,0:T(8,128)(2,1)}, f32[10...) custom-call(bf16[1024,768]{1,0:T(8,128)(2,1)} %get-tuple-element.43.att_ref.right0, ...), custom_call_target="tpu_custom_call" | custom-call | flops 14495514624 | bytes 44071936 | tf_op jit(solution)/shard_map/pallas_call | solution.py:63
  198.4 22.7 %shard_map.198 = (bf16[1024,768]{1,0:T(8,128)(2,1)}, f32[1024,768]{1,0:T(8,128)}) custom-call(bf16[1024,2304]{1,0:T(8,128)(2,1)} %get-tuple-element.44.q_ref.k_ref.v_ref, bf16[1024,2304]{1,0:T(8,128)(2,1)} %get-tuple-element.44.q_ref.k_ref.v_ref, bf16[1024,2304]{1,0:T(8,128)(2,1)} %get-tuple-element.44.q_ref.k_ref.v_ref, ...), custom_call_target="tpu_custom_call" | custom-call | flops 3221225472 | bytes 18882560 | tf_op jit(solution)/shard_map/pallas_call | solution.py:63
  221.2 35.6 %shard_map.199 = (bf16[1024,768]{1,0:T(8,128)(2,1)}, bf16[1024,768]{1,0:T(8,128)(2,1)}, bf16[1024,3072]{1,0:T(8,128)(2,1)}, bf16[1024,768]{1,0:T(8,128)(2,1)}, b...) custom-call(bf16[1024,768]{1,0:T(8,128)(2,1)} %get-tuple-element.45., ...), custom_call_target="tpu_custom_call" | custom-call | flops 21743271936 | bytes 42127360 | tf_op jit(solution)/shard_map/pallas_call | solution.py:63
  256.8 39.2 %shard_map.200.mgrad_ref.left1 = bf16[3,1024,768]{2,1,0:T(8,128)(2,1)} custom-call(bf16[1024,2304]{1,0:T(8,128)(2,1)} %get-tuple-element.44.q_ref.k_ref.v_ref, bf16[1024,2304]{1,0:T(8,128)(2,1)} %get-tuple-element.44.q_ref.k_ref.v_ref, bf16[1024,2304]{1,0:T(8,128)(2,1)} %get-tuple-element.44.q_ref.k_ref.v_ref, bf16[1024,768]{1,0:T(8,128)(2,1)} %get-tuple-element.48.grad_ref, ...), custom_call_target="tpu_custom_call" | custom-call | flops 8053063680 | bytes 25169920 | tf_op jit(solution)/shard_map/pallas_call | solution.py:63
  295.9 30.1 %shard_map.201 = (bf16[1024,768]{1,0:T(8,128)(2,1)}, bf16[1024,3072]{1,0:T(8,128)(2,1)}, bf16[1024,768]{1,0:T(8,128)(2,1)}, f32[1024,768]{1,0:T(8,128)}, bf16[1024,768]{1,0:T(8,128)(2,1)}, /*index=5*/f32[8,768]{1,0:T(8,128)}) custom-call(bf16[3,1024,768]{2,1,0:T(8,128)(2,1)} %shard_map.200.mgrad_ref.left1, f32[1024,768]{1,0:T(8,128)} %get-tuple-element.46.x_ref.later_ref, ...), custom_call_target="tpu_custom_call" | custom-call | flops 14495514624 | bytes 48812032 | tf_op jit(solution)/shard_map/pallas_call | solution.py:63
  326.1 6.1 shard_map.205
  332.3 39.2 %shard_map.202.mgrad_ref.left0 = bf16[3,1024,768]{2,1,0:T(8,128)(2,1)} custom-call(bf16[1024,2304]{1,0:T(8,128)(2,1)} %get-tuple-element.42.q_ref.k_ref.v_ref, bf16[1024,2304]{1,0:T(8,128)(2,1)} %get-tuple-element.42.q_ref.k_ref.v_ref, bf16[1024,2304]{1,0:T(8,128)(2,1)} %get-tuple-element.42.q_ref.k_ref.v_ref, bf16[1024,768]{1,0:T(8,128)(2,1)} %get-tuple-element.53.grad_ref, ...), custom_call_target="tpu_custom_call" | custom-call | flops 8053063680 | bytes 25169920 | tf_op jit(solution)/shard_map/pallas_call | solution.py:63
  371.5 12.2 %shard_map.204 = bf16[2304,768]{1,0:T(8,128)(2,1)} custom-call(bf16[3,1024,768]{2,1,0:T(8,128)(2,1)} %shard_map.202.mgrad_ref.left0, bf16[3,1024,768]{2,1,0:T(8,128)(2,1)} %shard_map.200.mgrad_ref.left1, bf16[1024,768]{1,0:T(8,128)(2,1)} %get-tuple-element.57.right0, bf16[1024,768]{1,0:T(8,128)(2,1)} %get-tuple-element.58.right1), custom_call_target="tpu_custom_call" | custom-call | flops 7247757312 | bytes 16121856 | tf_op jit(solution)/shard_map/pallas_call | solution.py:63
  383.7 26.2 %shard_map.206 = (bf16[3072,768]{1,0:T(8,128)(2,1)}, bf16[3072,768]{1,0:T(8,128)(2,1)}) custom-call(bf16[1024,3072]{1,0:T(8,128)(2,1)} %get-tuple-element.61.act0, bf16[1024,3072]{1,0:T(8,128)(2,1)} %get-tuple-element.62.act1, bf16[1024,3072]{1,0:T(8,128)(2,1)} %get-tuple-element.63.lift0, bf16[1024,3072]{1,0:T(8,128)(2,1)} %get-tuple-element.64.lift1, ...), custom_call_target="tpu_custom_call" | custom-call | flops 19327352832 | bytes 40894464 | tf_op jit(solution)/shard_map/pallas_call | solution.py:63
  410.6 9.8 %shard_map.203 = (f32[1024,768]{1,0:T(8,128)}, f32[8,768]{1,0:T(8,128)}) custom-call(bf16[3,1024,768]{2,1,0:T(8,128)(2,1)} %shard_map.202.mgrad_ref.left0, bf16[1024,768]{1,0:T(8,128)(2,1)} %bitcast.68, f32[1024,768]{1,0:T(8,128)} %get-tuple-element.55.hgrad_ref, f32[8,768]{1,0:T(8,128)} %broadcast_select_fusion.norms_ref, bf16[2304,768]{1,0:T(8,128)(2,1)} %bitcast.58), custom_call_target="tpu_custom_call" | custom-call | flops 3623878656 | bytes 16171008 | tf_op jit(solution)/shard_map/pallas_call | solution.py:63
  420.4 0.8 slice_add_fusion
  421.5 38.9 %all-reduce.2 = f32[9,768]{1,0:T(8,128)S(1)} all-reduce(f32[9,768]{1,0:T(8,128)S(1)} %concatenate.15), channel_id=7, replica_groups=mesh['dp'=4,'fsdp'=8] {'dp','fsdp'}, use_global_device_ids=true, to_apply=%region_5.6.clone | all-reduce | flops 6912 | bytes 55296
  462.3 1.4 convert_bitcast_fusion.2
  463.7 70.6 %reduce-scatter.6.cloned.1.call-done = bf16[72,768]{1,0:T(8,128)(2,1)} async-done(((bf16[2304,768]{1,0:T(8,128)(2,1)}), bf16[72,768]{1,0:T(8,128)(2,1)}) %reduce-scatter.6.cloned.1.call-update) | async-done | bytes 110608 | tf_op jit(solution)/shard_map/reduce_scatter | solution.py:608
  534.3 1.6 convert_bitcast_fusion.1
  535.9 109.6 %reduce-scatter.10.cloned.1.call-done = bf16[96,768]{1,0:T(8,128)(2,1)} async-done(((bf16[3072,768]{1,0:T(8,128)(2,1)}), bf16[96,768]{1,0:T(8,128)(2,1)}) %reduce-scatter.10.cloned.1.call-update) | async-done | bytes 147472 | tf_op jit(solution)/shard_map/reduce_scatter | solution.py:608
  645.5 1.6 convert_bitcast_fusion
  647.1 110.7 %reduce-scatter.12.cloned.1.call-done = bf16[96,768]{1,0:T(8,128)(2,1)} async-done(((bf16[3072,768]{1,0:T(8,128)(2,1)}), bf16[96,768]{1,0:T(8,128)(2,1)}) %reduce-scatter.12.cloned.1.call-update) | async-done | bytes 147472 | tf_op jit(solution)/shard_map/reduce_scatter | solution.py:608
  757.8 1.6 convert_element_type.23
  (40 shorter events, 7.7 us)
Async XLA Ops:
  7.2 114.7 %all-gather.3.cloned.1.call-start = ((), (), s32[]{:S(2)}) async-start(), calls=%async_computation.8 | async-start | bytes 15409152 | tf_op jit(solution)/shard_map/all_gather | solution.py:504
  12.4 449.9 %reduce-scatter.8.cloned.1.call-start = ((), (), s32[]{:S(2)}) async-start(), calls=%async_computation.5 | async-start | bytes 1216512 | tf_op jit(solution)/shard_map/reduce_scatter | solution.py:608
  134.9 3.6 copy-start.1
  332.2 202.1 %reduce-scatter.6.cloned.1.call-start = ((), (), s32[]{:S(2)}) async-start(), calls=%async_computation.4 | async-start | bytes 3649536 | tf_op jit(solution)/shard_map/reduce_scatter | solution.py:608
  383.7 261.8 %reduce-scatter.10.cloned.1.call-start = ((), (), s32[]{:S(2)}) async-start(), calls=%async_computation.6 | async-start | bytes 4866048 | tf_op jit(solution)/shard_map/reduce_scatter | solution.py:608
  410.0 347.8 %reduce-scatter.12.cloned.1.call-start = ((), (), s32[]{:S(2)}) async-start(), calls=%async_computation.7 | async-start | bytes 4866048 | tf_op jit(solution)/shard_map/reduce_scatter | solution.py:608
  410.6 9.8 %copy-start = (f32[8,768]{1,0:T(8,128)S(1)}, f32[8,768]{1,0:T(8,128)}, u32[]{:S(2)}) copy-start(f32[8,768]{1,0:T(8,128)} %get-tuple-element.71) | copy-start | bytes 73732
Sparse Core Ops, SparseCore 0:
  12.5 109.3 all-gather.2
  332.3 94.2 reduce-scatter.7
  432.1 102.1 reduce-scatter.5
  539.6 105.8 reduce-scatter.9
  651.7 106.0 reduce-scatter.11
